TPU v7x, 32 devices: a whole 2x2x4 slice. The times are simulated.
32 devices in a mesh: grp: 2 (over y), row: 4 (over z), col: 2 (over x), sub: 2 (over core).
Axes of the slice: x: 2, y: 2, z: 4, core: 2. Of those that a mesh axis runs over, the one named last changes fastest.
Arguments:
- features: bfloat16 [5120, 64], P(('grp', 'row', 'col', 'sub')), parts along dimension 0, may hold values from -6 to 6
- probes: bfloat16 [5120, 33], P(('grp', 'row', 'col', 'sub')), parts along dimension 0, may hold values from -6 to 6
- tile_live: int32 [10], P('grp'), parts along dimension 0, may hold values from 1 to 512, 1920 in all
- lengthscale: float32 [2], P('grp'), parts along dimension 0, may hold values from 3 to 5
Outputs:
- kernel_product: float32 [5120, 33], P(('grp', 'row', 'col', 'sub')), parts along dimension 0
- derivative_product: float32 [5120, 33], P(('grp', 'row', 'col', 'sub')), parts along dimension 0
There are 2 independent parts, one for each index of `grp`. A program takes and returns all parts, laid end to end along the dimension named above; each array names one. Nothing has to cross between parts.
Inputs may be any that keep to these rules, and one draw needn't show every extreme that they name: Tile t holds evaluated designs in its first tile_live[t] slots; the counts sum to 1920 and at least one tile is full.
All inputs are finite; a program needn't handle non-finite values.
Results may differ from a plain program's by a relative error of at most 0.0003.
Values may be sent and summed in bfloat16 or wider, within the bound.
A program may use at most 64 MiB of HBM per device.

v0:
```python
import math

import jax
import jax.numpy as jnp
from jax import lax
from jax.sharding import PartitionSpec as P

TILE = 512


ROOT_FIVE = math.sqrt(5.0)
HIGH = lax.Precision.HIGHEST


def row_norms(feat):
    feat_float = feat.astype(jnp.float32)
    return jnp.sum(feat_float * feat_float, axis=1)


def kernel_pair(left_feat, left_norms, right_feat, right_norms, inv_length):
    cross = lax.dot_general(
        left_feat, right_feat, (((1,), (1,)), ((), ())), preferred_element_type=jnp.float32
    )
    dist_sq = jnp.maximum(left_norms[:, None] + right_norms[None, :] - 2.0 * cross, 0.0)
    scaled = ROOT_FIVE * inv_length * jnp.sqrt(dist_sq)
    decay = jnp.exp(-scaled)
    kmat = (1.0 + scaled + scaled * scaled / 3.0) * decay
    dmat = scaled * scaled * (1.0 + scaled) * decay * (inv_length / 3.0)
    return (kmat, dmat)


def per_device(features, probes, tile_live, lengthscale):
    shard_rows = features.shape[0]
    width_probe = probes.shape[1]
    inv_length = 1.0 / lengthscale[0]
    factor = 4.0 / math.sqrt(shard_rows * lax.axis_size(("row", "col", "sub")))
    place_index = lax.axis_index(("row", "col", "sub"))
    global_rows = place_index * shard_rows + jnp.arange(shard_rows, dtype=jnp.int32)
    tile_index = global_rows // TILE
    tile_ids = jnp.arange(tile_live.shape[0], dtype=jnp.int32)
    live_count = jnp.sum(
        jnp.where(tile_index[:, None] == tile_ids[None, :], tile_live[None, :], 0), axis=1
    )
    live_rows = global_rows % TILE < live_count
    live_float = (live_rows.astype(jnp.float32) * factor)[:, None]
    masked = probes * live_rows.astype(jnp.bfloat16)[:, None]
    block_feat, block_vals = (
        lax.all_gather(features, ("col", "sub"), axis=0, tiled=True),
        lax.all_gather(masked, ("col", "sub"), axis=0, tiled=True),
    )
    block_norms = row_norms(block_feat)
    block_float = block_vals.astype(jnp.float32)
    group_count = lax.axis_size(("col", "sub"))
    stripe_count = lax.axis_size("row")
    row_index = lax.axis_index("row")
    col_index = lax.axis_index(("col", "sub"))
    piece_ids = jnp.arange(group_count, dtype=jnp.int32)

    def weights(source):
        left_place = row_index * group_count + piece_ids
        right_place = source * group_count + col_index
        direct = left_place <= right_place
        transposed = left_place < right_place
        return (direct.astype(jnp.float32), transposed.astype(jnp.float32))

    row_empty = jnp.zeros((group_count * shard_rows, width_probe), jnp.float32)
    col_empty = jnp.zeros((stripe_count * shard_rows, width_probe), jnp.float32)
    piece_feat = lax.all_gather(features, "row", axis=0, tiled=True)
    piece_vals = lax.all_gather(masked, "row", axis=0, tiled=True)
    total = piece_feat.shape[0]
    width = min(total, shard_rows)

    def advance(counter, totals):
        offset = counter * width
        direct_w, trans_w = weights(offset // shard_rows)

        def compute(kept):
            col_feat = lax.dynamic_slice_in_dim(piece_feat, counter * width, width, 0)
            col_vals = lax.dynamic_slice_in_dim(piece_vals, counter * width, width, 0).astype(
                jnp.float32
            )
            col_norms = row_norms(col_feat)
            kmat, dmat = kernel_pair(block_feat, block_norms, col_feat, col_norms, inv_length)
            direct_rows = jnp.repeat(direct_w, shard_rows)[:, None]
            trans_rows = jnp.repeat(trans_w, shard_rows)[:, None]
            weighted = block_float * trans_rows
            new_kern = kept[0] + jnp.dot(kmat, col_vals, precision=HIGH) * direct_rows
            new_deriv = kept[1] + jnp.dot(dmat, col_vals, precision=HIGH) * direct_rows
            back_kern = lax.dot_general(kmat, weighted, (((0,), (0,)), ((), ())), precision=HIGH)
            back_deriv = lax.dot_general(dmat, weighted, (((0,), (0,)), ((), ())), precision=HIGH)
            col_kern = lax.dynamic_update_slice_in_dim(
                kept[2], lax.dynamic_slice_in_dim(kept[2], offset, width, 0) + back_kern, offset, 0
            )
            col_deriv = lax.dynamic_update_slice_in_dim(
                kept[3], lax.dynamic_slice_in_dim(kept[3], offset, width, 0) + back_deriv, offset, 0
            )
            return (new_kern, new_deriv, col_kern, col_deriv)

        return lax.cond(jnp.sum(direct_w) > 0.0, compute, lambda kept: kept, totals)

    kern_rows, deriv_rows, kern_cols, deriv_cols = lax.fori_loop(
        0, total // width, advance, (row_empty, row_empty, col_empty, col_empty)
    )
    kern_part, deriv_part = (
        lax.psum_scatter(kern_rows, ("col", "sub"), scatter_dimension=0, tiled=True),
        lax.psum_scatter(deriv_rows, ("col", "sub"), scatter_dimension=0, tiled=True),
    )
    kern_back, deriv_back = (
        lax.psum_scatter(kern_cols, "row", scatter_dimension=0, tiled=True),
        lax.psum_scatter(deriv_cols, "row", scatter_dimension=0, tiled=True),
    )
    return ((kern_part + kern_back) * live_float, (deriv_part + deriv_back) * live_float)


def solution(mesh):
    in_specs = (
        P(("grp", "row", "col", "sub"), None),
        P(("grp", "row", "col", "sub"), None),
        P("grp"),
        P("grp"),
    )
    out_specs = (P(("grp", "row", "col", "sub"), None), P(("grp", "row", "col", "sub"), None))
    return jax.shard_map(
        per_device, mesh=mesh, in_specs=in_specs, out_specs=out_specs, check_vma=False
    )
```

profile of v0, /device:TPU:0, one launch (start us, length us, event | category | flops | bytes accessed | tf_op | source)
XLA Modules:
  0.0 165.9 jit_solution(13820164066518008708)
XLA Ops:
  7.3 0.6 copy-done.2
  8.0 6.2 %all-gather.3 = bf16[4,160,33]{1,2,0:T(8,128)(2,1)S(1)} all-gather(bf16[1,160,33]{1,2,0:T(8,128)(2,1)S(1)} %multiply_bitcast_fusion), channel_id=1, replica_groups=mesh['grp'=2,'row'=4,'col'=2,'sub'=2] {'col','sub'}, dimensions={0}, use_global_device_ids=true | all-gather | bytes 52800 | tf_op jit(solution)/shard_map/all_gather | solution.py:49
  14.2 14.1 %all-gather.2 = bf16[4,160,33]{1,2,0:T(8,128)(2,1)S(1)} all-gather(bf16[1,160,33]{1,2,0:T(8,128)(2,1)S(1)} %multiply_bitcast_fusion), channel_id=1, replica_groups=mesh['grp'=2,'row'=4,'col'=2,'sub'=2] {'row'}, dimensions={0}, use_global_device_ids=true | all-gather | bytes 52800 | tf_op jit(solution)/shard_map/all_gather | solution.py:69
  28.3 5.4 %all-gather = bf16[4,160,64]{1,2,0:T(8,128)(2,1)S(1)} all-gather(bf16[1,160,64]{1,2,0:T(8,128)(2,1)S(1)} %bitcast.27), channel_id=1, replica_groups=mesh['grp'=2,'row'=4,'col'=2,'sub'=2] {'col','sub'}, dimensions={0}, use_global_device_ids=true | all-gather | bytes 102400 | tf_op jit(solution)/shard_map/all_gather | solution.py:48
  34.2 13.4 %all-gather.1 = bf16[4,160,64]{1,2,0:T(8,128)(2,1)S(1)} all-gather(bf16[1,160,64]{1,2,0:T(8,128)(2,1)S(1)} %bitcast.28), channel_id=1, replica_groups=mesh['grp'=2,'row'=4,'col'=2,'sub'=2] {'row'}, dimensions={0}, use_global_device_ids=true | all-gather | bytes 102400 | tf_op jit(solution)/shard_map/all_gather | solution.py:68
  48.8 23.1 %while.22 = (s32[]{:T(128)}, f32[640,33]{0,1:T(8,128)S(1)}, f32[640,33]{0,1:T(8,128)S(1)}, f32[640,33]{0,1:T(8,128)S(1)}, f32[640,33]{0,1:T(8,128)S(1)}, /*index...) while((s32[]{:T(128)}, f32[640,33]{0,1:T(8,128)S(1)}, ...), condition=%wide.region_7.8_spmd.clone, body=%wide.region_2.7_spmd.clone.sunk | while | flops 178446288 | bytes 3102029 | solution.py:101
  48.8 0.7 fusion.39
  50.2 4.3 %conditional.3 = ((f32[640,33]{0,1:T(8,128)S(1)}, f32[640,33]{0,1:T(8,128)S(1)}, f32[640,33]{0,1:T(8,128)S(1)}, f32[640,33]{0,1:T(8,128)S(1)})) conditional(s32[]{:T(128)} %convert_element_type.63, (f32[640,33]{0,1:T(8,128)S(1)}, f32[640,33]{0,1:T(8,128)S(1)}, f32[640,33]{0,1:T(8,128)S(1)}, f32[640,33]{0,1:T(8,128)S(1)}) %tuple.61, (f32[]{:T(128)}, ...), branch_computations={%region_4.4_spmd, %region_5.6_spmd} | conditional | flops 178446240 | bytes 3101532 | solution.py:99
  50.8 0.8 convolution_add_fusion
  51.6 0.5 dynamic_update_slice.5
  52.1 0.8 convolution_add_fusion.1
  53.0 0.5 dynamic_update_slice.4
  54.0 0.4 fusion.7
  54.5 0.7 fusion.39
  55.8 4.6 %conditional.3 = ((f32[640,33]{0,1:T(8,128)S(1)}, f32[640,33]{0,1:T(8,128)S(1)}, f32[640,33]{0,1:T(8,128)S(1)}, f32[640,33]{0,1:T(8,128)S(1)})) conditional(s32[]{:T(128)} %convert_element_type.63, (f32[640,33]{0,1:T(8,128)S(1)}, f32[640,33]{0,1:T(8,128)S(1)}, f32[640,33]{0,1:T(8,128)S(1)}, f32[640,33]{0,1:T(8,128)S(1)}) %tuple.61, (f32[]{:T(128)}, ...), branch_computations={%region_4.4_spmd, %region_5.6_spmd} | conditional | flops 178446240 | bytes 3101532 | solution.py:99
  56.5 0.8 convolution_add_fusion
  57.3 0.7 dynamic_update_slice.5
  58.0 0.8 convolution_add_fusion.1
  58.8 0.7 dynamic_update_slice.4
  60.0 0.4 fusion.7
  60.5 0.7 fusion.39
  61.8 4.5 %conditional.3 = ((f32[640,33]{0,1:T(8,128)S(1)}, f32[640,33]{0,1:T(8,128)S(1)}, f32[640,33]{0,1:T(8,128)S(1)}, f32[640,33]{0,1:T(8,128)S(1)})) conditional(s32[]{:T(128)} %convert_element_type.63, (f32[640,33]{0,1:T(8,128)S(1)}, f32[640,33]{0,1:T(8,128)S(1)}, f32[640,33]{0,1:T(8,128)S(1)}, f32[640,33]{0,1:T(8,128)S(1)}) %tuple.61, (f32[]{:T(128)}, ...), branch_computations={%region_4.4_spmd, %region_5.6_spmd} | conditional | flops 178446240 | bytes 3101532 | solution.py:99
  62.4 0.8 convolution_add_fusion
  63.2 0.6 dynamic_update_slice.5
  63.9 0.8 convolution_add_fusion.1
  64.7 0.6 dynamic_update_slice.4
  65.8 0.4 fusion.7
  66.3 0.7 fusion.39
  67.6 4.3 %conditional.3 = ((f32[640,33]{0,1:T(8,128)S(1)}, f32[640,33]{0,1:T(8,128)S(1)}, f32[640,33]{0,1:T(8,128)S(1)}, f32[640,33]{0,1:T(8,128)S(1)})) conditional(s32[]{:T(128)} %convert_element_type.63, (f32[640,33]{0,1:T(8,128)S(1)}, f32[640,33]{0,1:T(8,128)S(1)}, f32[640,33]{0,1:T(8,128)S(1)}, f32[640,33]{0,1:T(8,128)S(1)}) %tuple.61, (f32[]{:T(128)}, ...), branch_computations={%region_4.4_spmd, %region_5.6_spmd} | conditional | flops 178446240 | bytes 3101532 | solution.py:99
  68.3 0.8 convolution_add_fusion
  69.1 0.5 dynamic_update_slice.5
  69.6 0.8 convolution_add_fusion.1
  70.4 0.5 dynamic_update_slice.4
  71.1 0.4 fusion.8
  71.5 0.4 fusion.7
  71.9 0.9 copy.29
  72.9 0.9 copy.31
  73.8 0.9 copy.33
  74.8 0.9 copy.35
  75.7 15.9 %reduce-scatter.13.cloned.1.call-done = f32[160,33]{1,0:T(8,128)} async-done(((f32[640,33]{1,0:T(8,128)}), f32[160,33]{1,0:T(8,128)}) %reduce-scatter.13.cloned.1.call-update) | async-done | bytes 21136
  91.6 1.0 copy.30
  92.6 21.5 %reduce-scatter.15.cloned.1.call-done = f32[160,33]{1,0:T(8,128)} async-done(((f32[640,33]{1,0:T(8,128)}), f32[160,33]{1,0:T(8,128)}) %reduce-scatter.15.cloned.1.call-update) | async-done | bytes 21136
  114.1 1.0 copy.32
  115.0 20.5 %reduce-scatter.17.cloned.1.call-done = f32[160,33]{1,0:T(8,128)} async-done(((f32[640,33]{1,0:T(8,128)}), f32[160,33]{1,0:T(8,128)}) %reduce-scatter.17.cloned.1.call-update) | async-done | bytes 21136
  135.5 1.0 copy.34
  136.5 21.3 %reduce-scatter.19.cloned.1.call-done = f32[160,33]{1,0:T(8,128)} async-done(((f32[640,33]{1,0:T(8,128)}), f32[160,33]{1,0:T(8,128)}) %reduce-scatter.19.cloned.1.call-update) | async-done | bytes 21136
  157.8 1.0 copy.36
  158.7 0.7 add_multiply_fusion.3
  (60 shorter events, 5.6 us)
Async XLA Ops:
  7.2 0.8 copy-start.1
  7.2 84.5 %reduce-scatter.13.cloned.1.call-start = ((), (), s32[]{:S(2)}) async-start(), calls=%async_computation.4 | async-start | bytes 409600
  7.2 0.7 copy-start.2
  14.2 14.1 %copy-start = (bf16[160,64]{0,1:T(8,128)(2,1)S(1)}, bf16[160,64]{0,1:T(8,128)(2,1)}, u32[]{:S(2)}) copy-start(bf16[160,64]{0,1:T(8,128)(2,1)} %param.8) | copy-start | bytes 61444
  72.8 41.3 %reduce-scatter.15.cloned.1.call-start = ((), (), s32[]{:S(2)}) async-start(), calls=%async_computation.5 | async-start | bytes 409600
  73.8 61.7 %reduce-scatter.17.cloned.1.call-start = ((), (), s32[]{:S(2)}) async-start(), calls=%async_computation.6 | async-start | bytes 409600
  74.8 83.0 %reduce-scatter.19.cloned.1.call-start = ((), (), s32[]{:S(2)}) async-start(), calls=%async_computation.7 | async-start | bytes 409600
Sparse Core Ops, SparseCore 0:
  72.9 18.6 reduce-scatter.12
  94.0 20.0 reduce-scatter.14
  116.7 18.7 reduce-scatter.16
  137.6 20.0 reduce-scatter.18
where the time goes:
time: 166 us
  waiting for transfers between devices  79.2 us (48%)
  blocking collectives  39 us (23%)
  local copies, waits for them, and re-layouts  14.9 us (9%)
  between operations  14.6 us (9%)
  matrix products  10.9 us (7%)
  other arithmetic  3.97 us (2%)
  loops' own time  3.15 us (2%)
    unnamed x8, waiting for transfers between devices  79.2 us
    all_gather x1, blocking collectives, per_device(): piece_vals = lax.all_gather(masked, 'row', axis=0, tiled=True)  14.1 us
    all_gather x1, blocking collectives, per_device(): piece_feat = lax.all_gather(features, 'row', axis=0, tiled=True)  13.4 us
    unnamed x19, local copies, waits for them, and re-layouts  8.92 us
    all_gather x1, blocking collectives, per_device(): lax.all_gather(masked, ('col', 'sub'), axis=0, tiled=True)  6.21 us
    all_gather x1, blocking collectives, per_device(): lax.all_gather(features, ('col', 'sub'), axis=0, tiled=True)  5.41 us
  transfers between devices with their start and end apart: 4, of which 4 were waited for; matrix products, arithmetic and copies ran while one was open for 3% of the time, Pallas kernels for 0%

commit v1 on v0

v1 whole, which is shorter than its diff:
```python
import functools
import math

import jax
import jax.numpy as jnp
from jax import lax
from jax.experimental import pallas as pl
from jax.experimental.pallas import tpu as pltpu
from jax.sharding import PartitionSpec as P

TILE = 512
LANES = 128
MESH = pl.DeviceIdType.MESH
LN2 = math.log(2.0)
TINY = 1e-30


def partner(index, step, size):
    if size & (size - 1):
        return lax.rem(index + step, size)
    other = index
    bit = 1
    while bit < size:
        if step & bit:
            other = other + bit - 2 * bit * lax.rem(lax.div(index, bit), 2)
        bit *= 2
    return other


def source(index, step, size):
    if size & (size - 1):
        return lax.rem(index - step + size, size)
    return partner(index, step, size)


def kernel(
    sizes,
    live_ref, length_ref, feat_ref, probe_ref,
    kern_ref, deriv_ref,
    flip, left, held,
    z_send, z_recv, x_send, x_recv, s_send, s_recv,
):
    rows, cols, total = sizes
    width, shard = feat_ref.shape
    probes = probe_ref.shape[0]
    tiles = live_ref.shape[0]
    padded = flip.shape[1]
    z, x, s = lax.axis_index("row"), lax.axis_index("col"), lax.axis_index("sub")
    grp = lax.axis_index("grp")
    z_peer = [partner(z, m, rows) for m in range(rows)]
    z_from = [source(z, m, rows) for m in range(rows)]
    x_peer = [partner(x, m, cols) for m in range(cols)]
    x_from = [source(x, m, cols) for m in range(cols)]

    def slot(zz, xx, ss):
        begin = ((zz * cols + xx) * 2 + ss) * shard
        return held.at[pl.ds(pl.multiple_of(begin, 32), shard)]

    barrier = pltpu.get_barrier_semaphore()
    targets = [(grp, z_peer[m], x, s) for m in range(1, rows)]
    targets += [(grp, z, x_peer[m], s) for m in range(1, cols)]
    targets += [(grp, z, x, 1 - s)]
    for target in targets:
        pl.semaphore_signal(barrier, inc=1, device_id=target, device_id_type=MESH)

    first = ((z * cols + x) * 2 + s) * shard
    slots = first + lax.broadcasted_iota(jnp.int32, (1, shard), 1)
    live = jnp.zeros((1, shard), jnp.float32)
    for step in range((shard - 2) // TILE + 2):
        tile = lax.div(first, TILE) + step
        inside = slots - tile * TILE
        count = live_ref[jnp.minimum(tile, tiles - 1)]
        live = jnp.where((inside >= 0) & (inside < TILE) & (inside < count), 1.0, live)
    feat = feat_ref[...].astype(jnp.float32)
    norm = jnp.sum(feat * feat, axis=0, keepdims=True)
    high = norm.astype(jnp.bfloat16).astype(jnp.float32)
    middle = (norm - high).astype(jnp.bfloat16).astype(jnp.float32)
    low = norm - high - middle
    ones = jnp.ones((1, shard), jnp.float32)
    base = width + probes
    flip[...] = jnp.zeros_like(flip)
    flip[:width, :shard] = feat
    flip[width:base, :shard] = probe_ref[...].astype(jnp.float32) * live
    for place, row in enumerate((high, middle, low, ones, ones, ones)):
        flip[base + place : base + place + 1, :shard] = row
    mine = slot(z, x, s)
    mine[...] = flip[...].T[:shard].astype(jnp.bfloat16)

    pl.semaphore_wait(barrier, len(targets))

    started = []

    def send(block, send_sem, recv_sem, target):
        copy = pltpu.make_async_remote_copy(
            src_ref=block, dst_ref=block, send_sem=send_sem, recv_sem=recv_sem,
            device_id=target, device_id_type=MESH,
        )
        copy.start()
        started.append(copy)

    def landed(block, send_sem, recv_sem):
        pltpu.make_async_remote_copy(
            src_ref=block, dst_ref=block, send_sem=send_sem, recv_sem=recv_sem,
            device_id=(grp, z, x, 1 - s), device_id_type=MESH,
        ).wait_recv()

    def send_x(m, block):
        for n in range(1, cols):
            send(block, x_send.at[m, n], x_recv.at[m, n], (grp, z, x_peer[n], s))

    def send_s(m, n, block):
        send(block, s_send.at[m, n], s_recv.at[m, n], (grp, z, x, 1 - s))

    send_x(0, mine)
    for m in range(1, rows):
        send(mine, z_send.at[m], z_recv.at[m], (grp, z_peer[m], x, s))
    send_s(0, 0, mine)

    flip[:width, :shard] = -2.0 * feat
    flip[width:base, :shard] = jnp.zeros((probes, shard), jnp.float32)
    for place, row in enumerate((ones, ones, ones, high, middle, low)):
        flip[base + place : base + place + 1, :shard] = row
    left[...] = flip[...].T[:shard].astype(jnp.bfloat16)

    inv = 1.0 / length_ref[0]
    gain = 5.0 * inv * inv / (LN2 * LN2)
    span = 640 if (cols * 2 * shard) % 640 == 0 else shard

    def chunk(begin, sums):
        block = held[pl.ds(pl.multiple_of(begin, 32), span), :]
        dist = lax.dot_general(
            left[...], block, (((1,), (1,)), ((), ())), preferred_element_type=jnp.float32
        )
        square = jnp.maximum(dist * gain, TINY)
        depth = square * lax.rsqrt(square)
        decay = jnp.exp2(-depth)
        kmat = (1.0 + depth * (LN2 + depth * (LN2 * LN2 / 3.0))) * decay
        dmat = square * decay * (1.0 + LN2 * depth)
        done = []
        for mat, kept in zip((kmat, dmat), sums):
            top = mat.astype(jnp.bfloat16)
            rest = (mat - top.astype(jnp.float32)).astype(jnp.bfloat16)
            done.append(
                kept
                + jnp.dot(top, block, preferred_element_type=jnp.float32)
                + jnp.dot(rest, block, preferred_element_type=jnp.float32)
            )
        return tuple(done)

    def compute(m, sums):
        plane = z_from[m] * (cols * 2 * shard)
        pieces = cols * 2 * shard // span
        if pieces == 1:
            return chunk(plane, sums)
        return lax.fori_loop(0, pieces, lambda p, kept: chunk(plane + p * span, kept), sums)

    empty = jnp.zeros((shard, LANES), jnp.float32)
    sums = (empty, empty)
    for m in range(rows):
        if m + 1 < rows:
            block = slot(z_from[m + 1], x, s)
            landed(block, z_send.at[m + 1], z_recv.at[m + 1])
            send_x(m + 1, block)
            send_s(m + 1, 0, block)
        for n in range(1, cols):
            block = slot(z_from[m], x_from[n], s)
            landed(block, x_send.at[m, n], x_recv.at[m, n])
            send_s(m, n, block)
        for n in range(cols):
            landed(slot(z_from[m], x_from[n], 1 - s), s_send.at[m, n], s_recv.at[m, n])
        sums = compute(m, sums)

    factor = 4.0 / math.sqrt(total)
    for out, kept, scale in zip(
        (kern_ref, deriv_ref), sums, (factor, factor * LN2 * LN2 / 3.0 * inv)
    ):
        whole = jnp.concatenate([kept, jnp.zeros((padded - shard, LANES), jnp.float32)], axis=0)
        out[...] = whole.T[width:base, :shard] * (live * scale)
    for copy in started:
        copy.wait_send()


def solution(mesh):
    rows, cols = mesh.shape["row"], mesh.shape["col"]

    def per_device(features, probes, tile_live, lengthscale):
        shard, width = features.shape
        count = probes.shape[1]
        total = shard * rows * cols * 2
        padded = (shard + LANES - 1) // LANES * LANES
        out = jax.ShapeDtypeStruct((count, shard), jnp.float32)
        vmem, smem = pl.BlockSpec(memory_space=pltpu.VMEM), pl.BlockSpec(memory_space=pltpu.SMEM)
        dma = pltpu.SemaphoreType.DMA
        kern, deriv = pl.pallas_call(
            functools.partial(kernel, (rows, cols, total)),
            out_shape=(out, out),
            in_specs=[smem, smem, vmem, vmem],
            out_specs=(vmem, vmem),
            scratch_shapes=[
                pltpu.VMEM((LANES, padded), jnp.float32),
                pltpu.VMEM((shard, LANES), jnp.bfloat16),
                pltpu.VMEM((total, LANES), jnp.bfloat16),
                dma((rows,)), dma((rows,)),
                dma((rows, cols)), dma((rows, cols)),
                dma((rows, cols)), dma((rows, cols)),
            ],
            compiler_params=pltpu.CompilerParams(
                collective_id=0, has_side_effects=True, vmem_limit_bytes=48 << 20
            ),
        )(tile_live, lengthscale, features.T, probes.T)
        return kern.T, deriv.T

    split = P(("grp", "row", "col", "sub"), None)
    return jax.shard_map(
        per_device,
        mesh=mesh,
        in_specs=(split, split, P("grp"), P("grp")),
        out_specs=(split, split),
        check_vma=False,
    )
```

time: 166 us -> 22.9 us (0.14)
  waiting for transfers between devices: 79.2 us -> 0 us
  blocking collectives: 39 us -> 0 us
  Pallas kernels: 0 us -> 17.8 us
  between operations: 14.6 us -> 1.3 us
  local copies, waits for them, and re-layouts: 14.9 us -> 3.37 us
  matrix products: 10.9 us -> 0 us
  other arithmetic: 3.97 us -> 0 us
  loops' own time: 3.15 us -> 0 us
    unnamed x8 -> x0, waiting for transfers between devices: 79.2 us -> none
    all_gather x4 -> x0, blocking collectives: 39 us -> none  [the longest x1 14.1 us: per_device(): piece_vals = lax.all_gather(masked, 'row', axis=0, tiled=True)]
    pallas_call x0 -> x1, Pallas kernels: none -> 17.8 us  [per_device(): pl.pallas_call(functools.partial(kernel, (rows, cols, total)), out_shape=...]
    dot_general x20 -> x0, matrix products: 10.9 us -> none  [the longest x4 3.21 us: compute(): lax.dot_general(dmat, weighted, (((0,), (0,)), ((), ())), precision=HIGH)]
    unnamed x19 -> x8, local copies, waits for them, and re-layouts: 8.92 us -> 3.37 us
    dynamic_update_slice x8 -> x0, local copies, waits for them, and re-layouts: 4.62 us -> none  [the longest x4 2.31 us: compute(): lax.dynamic_update_slice_in_dim(kept[2], lax.dynamic_slice_in_dim(kept[2]...]
    reduce_sum x10 -> x0, other arithmetic: 3.26 us -> none  [the longest x4 2.66 us: advance(): return lax.cond(jnp.sum(direct_w) > 0.0, compute, lambda kept: kept, totals)]
    another operation x5 -> x0, loops' own time: 3.15 us -> none  [the longest x1 2.78 us: per_device(): lax.fori_loop(0, total // width, advance, (row_empty, row_empty, col_empt...]
  transfers between devices with their start and end apart: 4 -> 0, of which waited for: 4 -> 0; matrix products, arithmetic and copies ran while one was open for 3% -> 0% of each run, Pallas kernels for 0% -> 0%
where the time goes in v1:
time: 22.9 us; the launch traced here: 22.5 us
  Pallas kernels  17.8 us (78%)
  local copies, waits for them, and re-layouts  3.37 us (15%)
  between operations  1.3 us (6%)
    pallas_call x1, Pallas kernels, per_device(): pl.pallas_call(functools.partial(kernel, (rows, cols, total)), out_shape=...  17.8 us
    unnamed x8, local copies, waits for them, and re-layouts  3.37 us

profile of v1, /device:TPU:0, one launch (start us, length us, event | category | flops | bytes accessed | tf_op | source)
XLA Modules:
  0.0 22.5 jit_solution(12276952821030730291)
XLA Ops:
  1.3 0.0 copy-start.2
  1.3 0.6 %copy-done.2 = s32[5]{0:T(128)S(1)} copy-done((s32[5]{0:T(128)S(1)}, s32[5]{0:T(128)}, u32[]{:S(2)}) %copy-start.2) | copy-done | bytes 44
  1.9 0.0 copy-start
  1.9 0.8 %copy-done = bf16[160,64]{0,1:T(8,128)(2,1)S(1)} copy-done((bf16[160,64]{0,1:T(8,128)(2,1)S(1)}, bf16[160,64]{0,1:T(8,128)(2,1)}, u32[]{:S(2)}) %copy-start) | copy-done | bytes 20504
  2.7 0.0 copy-start.1
  2.7 0.7 %copy-done.1 = bf16[160,33]{0,1:T(8,128)(2,1)S(1)} copy-done((bf16[160,33]{0,1:T(8,128)(2,1)S(1)}, bf16[160,33]{0,1:T(8,128)(2,1)}, u32[]{:S(2)}) %copy-start.1) | copy-done | bytes 10584
  3.4 17.8 %shard_map.59 = (f32[33,160]{1,0:T(8,128)S(1)}, f32[33,160]{1,0:T(8,128)S(1)}) custom-call(s32[5]{0:T(128)S(1)} %copy-done.2, f32[1]{0:T(128)S(6)} %copy.8.length_ref, bf16[64,160]{1,0:T(8,128)(2,1)S(1)} %bitcast.6, bf16[33,160]{1,0:T(8,128)(2,1)S(1)} %bitcast.7), custom_call_target="tpu_custom_call" | custom-call | tf_op jit(solution)/shard_map/pallas_call | solution.py:194
  21.3 0.6 %copy.9 = f32[160,33]{0,1:T(8,128)} copy(f32[160,33]{0,1:T(8,128)S(1)} %bitcast.5) | data formatting | bytes 42240
  21.9 0.6 %copy.10 = f32[160,33]{0,1:T(8,128)} copy(f32[160,33]{0,1:T(8,128)S(1)} %bitcast.4) | data formatting | bytes 42240
Async XLA Ops:
  1.3 0.7 %copy-start.2 = (s32[5]{0:T(128)S(1)}, s32[5]{0:T(128)}, u32[]{:S(2)}) copy-start(s32[5]{0:T(128)} %live_ref.1) | copy-start | bytes 64
  1.9 0.8 %copy-start = (bf16[160,64]{0,1:T(8,128)(2,1)S(1)}, bf16[160,64]{0,1:T(8,128)(2,1)}, u32[]{:S(2)}) copy-start(bf16[160,64]{0,1:T(8,128)(2,1)} %param.4) | copy-start | bytes 61444
  2.7 0.7 %copy-start.1 = (bf16[160,33]{0,1:T(8,128)(2,1)S(1)}, bf16[160,33]{0,1:T(8,128)(2,1)}, u32[]{:S(2)}) copy-start(bf16[160,33]{0,1:T(8,128)(2,1)} %param.5) | copy-start | bytes 31684

commit v2 on v1

--- a/solution.py
+++ b/solution.py
@@ -35,12 +35,13 @@
 
 def kernel(
     sizes,
-    live_ref, length_ref, feat_ref, probe_ref,
-    kern_ref, deriv_ref,
+    live_hbm, length_hbm, feat_hbm, probe_hbm,
+    out_ref,
+    live_ref, length_ref, feat_ref, probe_ref, load_sem,
     flip, left, held,
-    z_send, z_recv, x_send, x_recv, s_send, s_recv,
+    x_send, x_recv, s_send, s_recv,
 ):
-    rows, cols, total = sizes
+    rows, cols = sizes
     width, shard = feat_ref.shape
     probes = probe_ref.shape[0]
     tiles = live_ref.shape[0]
@@ -53,15 +54,22 @@
     x_from = [source(x, m, cols) for m in range(cols)]
 
     def slot(zz, xx, ss):
-        begin = ((zz * cols + xx) * 2 + ss) * shard
+        begin = ((zz * 2 + ss) * cols + xx) * shard
         return held.at[pl.ds(pl.multiple_of(begin, 32), shard)]
 
     barrier = pltpu.get_barrier_semaphore()
-    targets = [(grp, z_peer[m], x, s) for m in range(1, rows)]
-    targets += [(grp, z, x_peer[m], s) for m in range(1, cols)]
+    steps = [(m, n) for m in reversed(range(rows)) for n in reversed(range(cols)) if m or n]
+    targets = [(grp, z_peer[m], x_peer[n], s) for m, n in steps]
     targets += [(grp, z, x, 1 - s)]
     for target in targets:
         pl.semaphore_signal(barrier, inc=1, device_id=target, device_id_type=MESH)
+    pairs = ((feat_hbm, feat_ref), (probe_hbm, probe_ref), (live_hbm, live_ref), (length_hbm, length_ref))
+    loads = [pltpu.make_async_copy(a, b, load_sem.at[k]) for k, (a, b) in enumerate(pairs)]
+    for load in loads:
+        load.start()
+    flip[...] = jnp.zeros_like(flip)
+    for load in loads:
+        load.wait()
 
     first = ((z * cols + x) * 2 + s) * shard
     slots = first + lax.broadcasted_iota(jnp.int32, (1, shard), 1)
@@ -78,7 +86,6 @@
     low = norm - high - middle
     ones = jnp.ones((1, shard), jnp.float32)
     base = width + probes
-    flip[...] = jnp.zeros_like(flip)
     flip[:width, :shard] = feat
     flip[width:base, :shard] = probe_ref[...].astype(jnp.float32) * live
     for place, row in enumerate((high, middle, low, ones, ones, ones)):
@@ -104,16 +111,11 @@
             device_id=(grp, z, x, 1 - s), device_id_type=MESH,
         ).wait_recv()
 
-    def send_x(m, block):
-        for n in range(1, cols):
-            send(block, x_send.at[m, n], x_recv.at[m, n], (grp, z, x_peer[n], s))
-
     def send_s(m, n, block):
         send(block, s_send.at[m, n], s_recv.at[m, n], (grp, z, x, 1 - s))
 
-    send_x(0, mine)
-    for m in range(1, rows):
-        send(mine, z_send.at[m], z_recv.at[m], (grp, z_peer[m], x, s))
+    for m, n in steps:
+        send(mine, x_send.at[m, n], x_recv.at[m, n], (grp, z_peer[m], x_peer[n], s))
     send_s(0, 0, mine)
 
     flip[:width, :shard] = -2.0 * feat
@@ -124,7 +126,8 @@
 
     inv = 1.0 / length_ref[0]
     gain = 5.0 * inv * inv / (LN2 * LN2)
-    span = 640 if (cols * 2 * shard) % 640 == 0 else shard
+    half = cols * shard
+    span = 2 * shard if cols % 2 == 0 else shard
 
     def chunk(begin, sums):
         block = held[pl.ds(pl.multiple_of(begin, 32), span), :]
@@ -147,35 +150,34 @@
             )
         return tuple(done)
 
-    def compute(m, sums):
-        plane = z_from[m] * (cols * 2 * shard)
-        pieces = cols * 2 * shard // span
+    def compute(m, ss, sums):
+        begin = (z_from[m] * 2 + ss) * half
+        pieces = half // span
         if pieces == 1:
-            return chunk(plane, sums)
-        return lax.fori_loop(0, pieces, lambda p, kept: chunk(plane + p * span, kept), sums)
+            return chunk(begin, sums)
+        return lax.fori_loop(0, pieces, lambda p, kept: chunk(begin + p * span, kept), sums)
+
+    def other_half(m, sums):
+        for n in range(cols):
+            landed(slot(z_from[m], x_from[n], 1 - s), s_send.at[m, n], s_recv.at[m, n])
+        return compute(m, 1 - s, sums)
 
     empty = jnp.zeros((shard, LANES), jnp.float32)
     sums = (empty, empty)
     for m in range(rows):
-        if m + 1 < rows:
-            block = slot(z_from[m + 1], x, s)
-            landed(block, z_send.at[m + 1], z_recv.at[m + 1])
-            send_x(m + 1, block)
-            send_s(m + 1, 0, block)
-        for n in range(1, cols):
-            block = slot(z_from[m], x_from[n], s)
-            landed(block, x_send.at[m, n], x_recv.at[m, n])
-            send_s(m, n, block)
         for n in range(cols):
-            landed(slot(z_from[m], x_from[n], 1 - s), s_send.at[m, n], s_recv.at[m, n])
-        sums = compute(m, sums)
-
-    factor = 4.0 / math.sqrt(total)
-    for out, kept, scale in zip(
-        (kern_ref, deriv_ref), sums, (factor, factor * LN2 * LN2 / 3.0 * inv)
-    ):
+            if m or n:
+                block = slot(z_from[m], x_from[n], s)
+                landed(block, x_send.at[m, n], x_recv.at[m, n])
+                send_s(m, n, block)
+        if m:
+            sums = other_half(m - 1, sums)
+        sums = compute(m, s, sums)
+    sums = other_half(rows - 1, sums)
+
+    for place, (kept, scale) in enumerate(zip(sums, (1.0, LN2 * LN2 / 3.0 * inv))):
         whole = jnp.concatenate([kept, jnp.zeros((padded - shard, LANES), jnp.float32)], axis=0)
-        out[...] = whole.T[width:base, :shard] * (live * scale)
+        out_ref[place] = whole.T[width:base, :shard] * (live * scale)
     for copy in started:
         copy.wait_send()
 
@@ -188,27 +190,32 @@
         count = probes.shape[1]
         total = shard * rows * cols * 2
         padded = (shard + LANES - 1) // LANES * LANES
-        out = jax.ShapeDtypeStruct((count, shard), jnp.float32)
-        vmem, smem = pl.BlockSpec(memory_space=pltpu.VMEM), pl.BlockSpec(memory_space=pltpu.SMEM)
+        out = jax.ShapeDtypeStruct((2, count, shard), jnp.float32)
+        vmem, hbm = pl.BlockSpec(memory_space=pltpu.VMEM), pl.BlockSpec(memory_space=pltpu.HBM)
         dma = pltpu.SemaphoreType.DMA
-        kern, deriv = pl.pallas_call(
-            functools.partial(kernel, (rows, cols, total)),
-            out_shape=(out, out),
-            in_specs=[smem, smem, vmem, vmem],
-            out_specs=(vmem, vmem),
+        both = pl.pallas_call(
+            functools.partial(kernel, (rows, cols)),
+            out_shape=out,
+            in_specs=[hbm] * 4,
+            out_specs=vmem,
             scratch_shapes=[
+                pltpu.SMEM(tile_live.shape, jnp.int32),
+                pltpu.SMEM(lengthscale.shape, jnp.float32),
+                pltpu.VMEM((width, shard), jnp.bfloat16),
+                pltpu.VMEM((count, shard), jnp.bfloat16),
+                dma((4,)),
                 pltpu.VMEM((LANES, padded), jnp.float32),
                 pltpu.VMEM((shard, LANES), jnp.bfloat16),
                 pltpu.VMEM((total, LANES), jnp.bfloat16),
-                dma((rows,)), dma((rows,)),
                 dma((rows, cols)), dma((rows, cols)),
                 dma((rows, cols)), dma((rows, cols)),
             ],
             compiler_params=pltpu.CompilerParams(
-                collective_id=0, has_side_effects=True, vmem_limit_bytes=48 << 20
+                collective_id=0, has_side_effects=True, vmem_limit_bytes=(64 << 20) - (64 << 10)
             ),
         )(tile_live, lengthscale, features.T, probes.T)
-        return kern.T, deriv.T
+        factor = 4.0 / math.sqrt(total)
+        return (both[0] * factor).T, (both[1] * factor).T
 
     split = P(("grp", "row", "col", "sub"), None)
     return jax.shard_map(

time: 22.9 us -> 20.2 us (0.88)
  local copies, waits for them, and re-layouts: 3.37 us -> 0 us
  other arithmetic: 0 us -> 1.44 us
  Pallas kernels: 17.8 us -> 17.3 us
    unnamed x8 -> x0, local copies, waits for them, and re-layouts: 3.37 us -> none
    transpose x0 -> x1, other arithmetic: none -> 1.44 us  [per_device(): return ((both[0] * factor).T, (both[1] * factor).T)]
    pallas_call x1, Pallas kernels: 17.8 us -> 17.3 us  [per_device(): pl.pallas_call(functools.partial(kernel, (rows, cols)), out_shape=out, in...]
where the time goes in v2:
time: 20.2 us; the launch traced here: 20 us
  Pallas kernels  17.3 us (86%)
  other arithmetic  1.44 us (7%)
  between operations  1.29 us (6%)
    pallas_call x1, Pallas kernels, per_device(): pl.pallas_call(functools.partial(kernel, (rows, cols)), out_shape=out, in...  17.3 us
    transpose x1, other arithmetic, per_device(): return ((both[0] * factor).T, (both[1] * factor).T)  1.44 us

profile of v2, /device:TPU:0, one launch (start us, length us, event | category | flops | bytes accessed | tf_op | source)
XLA Modules:
  0.0 20.0 jit_solution(3643291344574464700)
XLA Ops:
  1.3 17.3 %shard_map.59 = f32[2,33,160]{2,1,0:T(8,128)} custom-call(s32[5]{0:T(128)} %live_hbm.1, f32[1]{0:T(128)S(6)} %copy.6.length_hbm, bf16[64,160]{1,0:T(8,128)(2,1)} %bitcast.10, bf16[33,160]{1,0:T(8,128)(2,1)} %bitcast.11), custom_call_target="tpu_custom_call" | custom-call | tf_op jit(solution)/shard_map/pallas_call | solution.py:196
  18.5 1.4 %multiply_bitcast_fusion = (f32[160,33]{0,1:T(8,128)}, f32[160,33]{0,1:T(8,128)}) fusion(f32[2,33,160]{2,1,0:T(8,128)} %shard_map.59), kind=kLoop, calls=%fused_computation | loop fusion | flops 10560 | bytes 84480 | tf_op jit(solution)/shard_map/transpose | solution.py:218

commit v3 on v2

--- a/solution.py
+++ b/solution.py
@@ -58,7 +58,7 @@
         return held.at[pl.ds(pl.multiple_of(begin, 32), shard)]
 
     barrier = pltpu.get_barrier_semaphore()
-    steps = [(m, n) for m in reversed(range(rows)) for n in reversed(range(cols)) if m or n]
+    steps = [(m, n) for m in range(rows) for n in range(cols) if m or n]
     targets = [(grp, z_peer[m], x_peer[n], s) for m, n in steps]
     targets += [(grp, z, x, 1 - s)]
     for target in targets:

time: 20.2 us -> 19.4 us (0.960)
  Pallas kernels: 17.3 us -> 16.4 us
    pallas_call x1, Pallas kernels: 17.3 us -> 16.4 us  [per_device(): pl.pallas_call(functools.partial(kernel, (rows, cols)), out_shape=out, in...]
where the time goes in v3:
time: 19.4 us; the launch traced here: 19.1 us
  Pallas kernels  16.4 us (85%)
  other arithmetic  1.44 us (7%)
  between operations  1.29 us (7%)
    pallas_call x1, Pallas kernels, per_device(): pl.pallas_call(functools.partial(kernel, (rows, cols)), out_shape=out, in...  16.4 us
    transpose x1, other arithmetic, per_device(): return ((both[0] * factor).T, (both[1] * factor).T)  1.44 us

profile of v3, /device:TPU:0, one launch (start us, length us, event | category | flops | bytes accessed | tf_op | source)
XLA Modules:
  0.0 19.1 jit_solution(17823494471135896477)
XLA Ops:
  1.3 16.4 %shard_map.59 = f32[2,33,160]{2,1,0:T(8,128)} custom-call(s32[5]{0:T(128)} %live_hbm.1, f32[1]{0:T(128)S(6)} %copy.6.length_hbm, bf16[64,160]{1,0:T(8,128)(2,1)} %bitcast.10, bf16[33,160]{1,0:T(8,128)(2,1)} %bitcast.11), custom_call_target="tpu_custom_call" | custom-call | tf_op jit(solution)/shard_map/pallas_call | solution.py:196
  17.7 1.4 %multiply_bitcast_fusion = (f32[160,33]{0,1:T(8,128)}, f32[160,33]{0,1:T(8,128)}) fusion(f32[2,33,160]{2,1,0:T(8,128)} %shard_map.59), kind=kLoop, calls=%fused_computation | loop fusion | flops 10560 | bytes 84480 | tf_op jit(solution)/shard_map/transpose | solution.py:218
